TPU v7x, 128 devices: a whole 4x4x4 slice. The times are simulated.
128 devices in a mesh: seq: 8 (over z_hi, x), tp: 16 (over y, z_lo, core).
Axes of the slice: x: 4, y: 4, z: 4 (z_hi: 2, z_lo: 2; z = z_hi * 2 + z_lo), core: 2. Of those that a mesh axis runs over, the one named last changes fastest.
Arguments:
- activations: bfloat16 [2048, 8192], P('seq', 'tp'), may hold values from -36 to 36
- norm_gain: bfloat16 [8192], P('tp'), may hold values from 0.099609375 to 1.8984375
- in_proj: bfloat16 [8192, 3, 4096], P(None, None, 'tp'), may hold values from -0.0625 to 0.0625
- short_taps: float32 [3, 3, 4096], P(None, None, 'tp'), may hold values from -3.5 to 3.5
- medium_taps: float32 [256, 128], P('tp'), may hold values from -0.5 to 0.5
- cotangent: bfloat16 [2048, 4096], P('seq', 'tp'), may hold values from -1.1953125 to 1.1953125
Outputs:
- mixer_out: bfloat16 [2048, 4096], P('seq', 'tp')
- grad_input: bfloat16 [2048, 8192], P('seq', 'tp')
- grad_proj: bfloat16 [8192, 3, 4096], P('seq', None, 'tp')
All inputs are finite; a program needn't handle non-finite values.
Results may differ from a plain program's by a relative error of at most 0.02.
Values may be sent and summed in bfloat16 or wider, within the bound.
A program may use at most 192 MiB of HBM per device.

v0:
```python
import jax
import jax.numpy as jnp
from jax import lax
from jax.sharding import PartitionSpec as P

GROUP = 16
LS = 3
LM = 128
norm_eps = 1e-06


def shifted(block, axis, distance):
    devices = range(lax.axis_size(axis))
    route = [(i - distance, i) for i in devices if i - distance in devices]
    return lax.ppermute(block, axis, route)


def forward_short(source, taps, offset, length):
    total = jnp.zeros((length,) + source.shape[1:], jnp.float32)
    for index in range(LS):
        total = total + taps[index] * source[offset - index : offset - index + length].astype(
            jnp.float32
        )
    return total


def backward_short(source, taps, length):
    total = jnp.zeros((length,) + source.shape[1:], jnp.float32)
    for index in range(LS):
        total = total + taps[index] * source[index : index + length].astype(jnp.float32)
    return total


def band_matrix(tap_rows, out_len, in_len, lead, sign):
    offsets = lead + sign * (
        lax.broadcasted_iota(jnp.int32, (out_len, in_len), 0)
        - lax.broadcasted_iota(jnp.int32, (out_len, in_len), 1)
    )
    inside = (offsets >= 0) & (offsets < LM)
    picked = jnp.take(tap_rows, jnp.clip(offsets, 0, LM - 1), axis=1)
    return jnp.where(inside[None], picked, 0.0)


def grouped_apply(band, source):
    groups_here = band.shape[0]
    shaped = source.astype(jnp.float32).reshape(source.shape[0], groups_here, GROUP)
    result = jnp.einsum("gts,sgc->tgc", band, shaped, precision=lax.Precision.HIGHEST)
    return result.reshape(band.shape[1], groups_here * GROUP)


def per_device(activations, norm_gain, in_proj, short_taps, medium_taps, cotangent):
    act_full, gain_full = (
        lax.all_gather(activations, "tp", axis=1, tiled=True),
        lax.all_gather(norm_gain, "tp", axis=0, tiled=True),
    )
    tok_rows = act_full.shape[0]
    width = act_full.shape[1]
    local_ch = in_proj.shape[2]
    edge_rows = LM + LS - 2
    head_rows = LS - 1
    act_float = act_full.astype(jnp.float32)
    inv_rms = lax.rsqrt(jnp.mean(act_float * act_float, axis=1, keepdims=True) + norm_eps)
    gain_float = gain_full.astype(jnp.float32)
    normed = (act_float * inv_rms * gain_float).astype(jnp.bfloat16)
    weight = in_proj.reshape(width, 3 * local_ch)
    projected = (
        jnp.dot(normed, weight, preferred_element_type=jnp.float32)
        .astype(jnp.bfloat16)
        .reshape(tok_rows, 3, local_ch)
    )
    kv_tail = projected[tok_rows - edge_rows :, 1:, :].reshape(edge_rows, 2 * local_ch)
    q_tail = projected[tok_rows - head_rows :, 0, :].reshape(head_rows // 2, 2 * local_ch)
    received = shifted(jnp.concatenate([kv_tail, q_tail], 0), "seq", 1)
    kv_ext = jnp.concatenate(
        [received[:edge_rows].reshape(edge_rows, 2, local_ch), projected[:, 1:, :]], 0
    )
    q_ext = jnp.concatenate(
        [received[edge_rows:].reshape(head_rows, local_ch), projected[:, 0, :]], 0
    )
    span = tok_rows + LM - 1
    kv_feat = forward_short(kv_ext, short_taps[:, 1:, :], head_rows, span).astype(jnp.bfloat16)
    q_feat = forward_short(q_ext, short_taps[:, 0, :], head_rows, tok_rows).astype(jnp.bfloat16)
    gated = (kv_feat[:, 0].astype(jnp.float32) * kv_feat[:, 1].astype(jnp.float32)).astype(
        jnp.bfloat16
    )
    band_forward = band_matrix(medium_taps, tok_rows, span, LM - 1, 1)
    filtered = grouped_apply(band_forward, gated)
    mixer_out = (q_feat.astype(jnp.float32) * filtered).astype(jnp.bfloat16)
    grad_out = cotangent.astype(jnp.float32)
    grad_filtered = (grad_out * q_feat.astype(jnp.float32)).astype(jnp.bfloat16)
    grad_q = (grad_out * filtered).astype(jnp.bfloat16)
    kv_own = kv_feat[LM - 1 :]
    front = jnp.concatenate([grad_q[:head_rows, None, :], kv_own[:head_rows]], 1)
    outgoing = jnp.concatenate(
        [grad_filtered[:edge_rows], front.reshape(3 * head_rows, local_ch)], 0
    )
    returned = shifted(outgoing, "seq", -1)
    filt_ext = jnp.concatenate([grad_filtered, returned[:edge_rows]], 0)
    front_next = returned[edge_rows:].reshape(head_rows, 3, local_ch)
    reach = tok_rows + head_rows
    band_backward = band_matrix(medium_taps, reach, tok_rows + edge_rows, 0, -1)
    grad_gated = grouped_apply(band_backward, filt_ext)
    kv_reach = jnp.concatenate([kv_own, front_next[:, 1:, :]], 0)
    q_reach = jnp.concatenate([grad_q, front_next[:, 0, :]], 0)
    grad_k = (grad_gated * kv_reach[:, 1].astype(jnp.float32)).astype(jnp.bfloat16)
    grad_v = (grad_gated * kv_reach[:, 0].astype(jnp.float32)).astype(jnp.bfloat16)
    grad_feat = jnp.stack([q_reach, grad_k, grad_v], 1)
    grad_pre = (
        backward_short(grad_feat, short_taps, tok_rows)
        .astype(jnp.bfloat16)
        .reshape(tok_rows, 3 * local_ch)
    )
    partial_grad = lax.dot_general(
        grad_pre, weight, (((1,), (1,)), ((), ())), preferred_element_type=jnp.float32
    )
    tp_count = lax.axis_size("tp")
    own_width = width // tp_count
    own_scaled = activations.astype(jnp.float32) * inv_rms
    own_gain = norm_gain.astype(jnp.float32)
    whole_grad = lax.psum(partial_grad.astype(jnp.bfloat16), "tp").astype(jnp.float32)
    stat = jnp.mean(gain_float * whole_grad * act_float, axis=1, keepdims=True) * inv_rms
    grad_slice = lax.dynamic_slice_in_dim(
        whole_grad, lax.axis_index("tp") * own_width, own_width, 1
    )
    grad_scaled = own_gain * grad_slice
    grad_input = (inv_rms * (grad_scaled - own_scaled * stat)).astype(jnp.bfloat16)
    row_share = width // lax.axis_size("seq")
    product = lax.dot_general(
        normed, grad_pre, (((0,), (0,)), ((), ())), preferred_element_type=jnp.float32
    )
    grad_proj = lax.psum_scatter(
        product.reshape(lax.axis_size("seq") * row_share, 3, local_ch).astype(jnp.bfloat16),
        "seq",
        scatter_dimension=0,
        tiled=True,
    )
    return (mixer_out, grad_input, grad_proj)


def solution(mesh):
    return jax.shard_map(
        per_device,
        mesh=mesh,
        in_specs=(
            P("seq", "tp"),
            P("tp"),
            P(None, None, "tp"),
            P(None, None, "tp"),
            P("tp", None),
            P("seq", "tp"),
        ),
        out_specs=(P("seq", "tp"), P("seq", "tp"), P("seq", None, "tp")),
        check_vma=False,
    )
```

profile of v0, /device:TPU:1, one launch (start us, length us, event | category | flops | bytes accessed | tf_op | source)
XLA Modules:
  0.0 847.9 jit_solution(10637052879910510053)
XLA Ops:
  8.6 21.9 %all-gather = bf16[16,1,512]{2,1,0:T(2,128)(2,1)S(1)} all-gather(bf16[1,1,512]{2,1,0:T(2,128)(2,1)S(1)} %reshape.189), channel_id=1, replica_groups=mesh['seq'=8,'tp'=16] {'tp'}, dimensions={0}, use_global_device_ids=true | all-gather | bytes 17408 | tf_op jit(solution)/shard_map/all_gather | solution.py:54
  30.5 16.7 %copy.82 = bf16[8192,3,256]{0,2,1:T(8,128)(2,1)} copy(bf16[8192,3,256]{2,0,1:T(8,128)(2,1)} %param.8) | data formatting | bytes 25165824 | tf_op args[2]
  48.0 179.6 %gather_fusion = f32[98048,16]{1,0:T(8,128)} fusion(f32[16,128]{0,1:T(8,128)S(1)} %copy.88, s32[98304]{0:T(1024)S(1)} %pad_clamp_fusion.1), kind=kCustom, calls=%fused_computation | custom fusion | bytes 12942336 | tf_op jit(solution)/shard_map/jit(_take)/gather | solution.py:40
  227.6 27.7 %copy.89 = f32[98048,16]{0,1:T(8,128)} copy(f32[98048,16]{1,0:T(8,128)} %gather_fusion) | data formatting | bytes 12550144 | tf_op jit(solution)/shard_map/jit(_take)/gather | solution.py:40
  255.3 10.9 %reshape.176 = f32[256,383,16]{1,0,2:T(8,128)} reshape(f32[98048,16]{0,1:T(8,128)} %copy.89) | data formatting | bytes 12550144 | tf_op jit(solution)/shard_map/jit(_take)/gather | solution.py:40
  267.0 182.5 %gather_fusion.1 = f32[99330,16]{1,0:T(8,128)} fusion(f32[16,128]{0,1:T(8,128)S(1)} %copy.88, s32[100352]{0:T(1024)S(1)} %pad_clamp_fusion), kind=kCustom, calls=%fused_computation.1 | custom fusion | bytes 13111560 | tf_op jit(solution)/shard_map/jit(_take)/gather | solution.py:40
  449.5 28.0 %copy.96 = f32[99330,16]{0,1:T(8,128)} copy(f32[99330,16]{1,0:T(8,128)} %gather_fusion.1) | data formatting | bytes 12714240 | tf_op jit(solution)/shard_map/jit(_take)/gather | solution.py:40
  477.5 15.4 %reshape.184 = f32[258,385,16]{1,0,2:T(8,128)} reshape(f32[99330,16]{0,1:T(8,128)} %copy.96) | data formatting | bytes 12714240 | tf_op jit(solution)/shard_map/jit(_take)/gather | solution.py:40
  493.2 3.1 fusion.5
  496.3 9.4 %convolution_convert_fusion.1 = bf16[256,768]{1,0:T(8,128)(2,1)S(1)} fusion(bf16[8192,768]{0,1:T(8,128)(2,1)} %bitcast.82, bf16[256,8192]{1,0:T(8,128)(2,1)} %all-gather.3.cloned.1.call-done, f32[8192]{0:T(1024)S(1)} %bitcast.95, f32[256]{0:T(256)S(1)} %add_rsqrt_fusion), kind=kOutput, calls=%fused_computation.31 | convolution fusion | flops 3229810688 | bytes 17204224 | tf_op jit(solution)/shard_map/dot_general | solution.py:67
  506.4 3.1 collective-permute-start
  509.6 2.8 collective-permute-done
  513.6 6.4 fusion.9
  520.9 1.3 collective-permute-start.1
  522.7 5.1 collective-permute-done.1
  528.5 8.0 fusion.1
  537.3 14.4 %fusion = bf16[256,8192]{1,0:T(8,128)(2,1)} fusion(bf16[256,3,256]{0,2,1:T(8,128)(2,1)S(1)} %add_convert_fusion, bf16[8192,3,256]{2,0,1:T(8,128)(2,1)} %param.8), kind=kOutput, calls=%fused_computation.7 | convolution fusion | flops 3223322624 | bytes 17170432 | tf_op jit(solution)/shard_map/dot_general | solution.py:113
  552.0 10.4 %convolution_convert_fusion = bf16[8192,3,256]{2,0,1:T(8,128)(2,1)} fusion(bf16[256,8192]{1,0:T(8,128)(2,1)} %all-gather.3.cloned.1.call-done, f32[8192]{0:T(1024)S(1)} %bitcast.96, f32[256]{0:T(256)S(1)} %add_rsqrt_fusion, bf16[256,3,256]{0,2,1:T(8,128)(2,1)S(1)} %add_convert_fusion), kind=kOutput, calls=%fused_computation.2 | convolution fusion | flops 3235905536 | bytes 17204224 | tf_op jit(solution)/shard_map/dot_general | solution.py:128
  563.9 120.6 %all-reduce.2.cloned.1.call-done = bf16[256,8192]{1,0:T(8,128)(2,1)} async-done(((bf16[256,8192]{1,0:T(8,128)(2,1)}), bf16[256,8192]{1,0:T(8,128)(2,1)}) %all-reduce.2.cloned.1.call-update) | async-done | bytes 4194320 | tf_op jit(solution)/shard_map/psum | solution.py:120
  684.5 3.3 convert_element_type.148
  687.9 1.3 copy-done.1
  689.2 1.7 fusion.8
  690.9 0.9 multiply_convert_fusion
  691.8 149.6 %reduce-scatter.2.cloned.1.call-done = bf16[1024,3,256]{2,0,1:T(8,128)(2,1)} async-done(((bf16[8192,3,256]{2,0,1:T(8,128)(2,1)}), bf16[1024,3,256]{2,0,1:T(8,128)(2,1)}) %reduce-scatter.2.cloned.1.call-update) | async-done | bytes 1572880 | tf_op jit(solution)/shard_map/reduce_scatter | solution.py:131
  (76 shorter events, 9.7 us)
Async XLA Ops:
  7.2 486.0 %all-gather.3.cloned.1.call-start = ((), (), s32[]{:S(2)}) async-start(), calls=%async_computation.1 | async-start | bytes 4456448 | tf_op jit(solution)/shard_map/all_gather | solution.py:53
  7.9 676.6 %all-reduce.2.cloned.1.call-start = ((), (), s32[]{:S(2)}) async-start(), calls=%async_computation.2 | async-start | bytes 8388608 | tf_op jit(solution)/shard_map/psum | solution.py:120
  30.5 16.8 %copy-start.5 = (f32[16,128]{1,0:T(8,128)S(1)}, f32[16,128]{1,0:T(8,128)}, u32[]{:S(2)}) copy-start(f32[16,128]{1,0:T(8,128)} %param.10) | copy-start | bytes 24580
  255.3 10.9 %copy-start.3 = (bf16[256,256]{1,0:T(8,128)(2,1)S(1)}, bf16[256,256]{1,0:T(8,128)(2,1)}, u32[]{:S(2)}) copy-start(bf16[256,256]{1,0:T(8,128)(2,1)} %param.11) | copy-start | bytes 393220
  477.5 15.6 %copy-start.4 = (f32[3,3,256]{2,1,0:T(4,128)S(1)}, f32[3,3,256]{2,1,0:T(4,128)}, u32[]{:S(2)}) copy-start(f32[3,3,256]{2,1,0:T(4,128)} %param.9) | copy-start | bytes 27652
  506.4 6.0 collective-permute-start
  520.9 6.9 collective-permute-start.1
  551.7 289.7 %reduce-scatter.2.cloned.1.call-start = ((), (), s32[]{:S(2)}) async-start(), calls=%async_computation.3 | async-start | bytes 14155776 | tf_op jit(solution)/shard_map/reduce_scatter | solution.py:131
  562.4 0.7 copy-start.6
  563.9 127.0 %copy-start.2 = (bf16[256,512]{1,0:T(8,128)(2,1)S(1)}, bf16[256,512]{1,0:T(8,128)(2,1)}, u32[]{:S(2)}) copy-start(bf16[256,512]{1,0:T(8,128)(2,1)} %param.6) | copy-start | bytes 786436
  684.5 3.4 copy-start
  684.5 4.7 copy-start.1
Sparse Core Ops, SparseCore 0:
  9.7 40.9 all-gather.2
  551.8 132.6 all-reduce.1
  689.0 152.3 reduce-scatter.1
where the time goes:
time: 849 us; the launch traced here: 848 us
  local copies, waits for them, and re-layouts  468 us (55%)
  waiting for transfers between devices  279 us (33%)
  matrix products  48.6 us (6%)
  blocking collectives  21.9 us (3%)
  between operations  14.1 us (2%)
  other arithmetic  12.1 us (1%)
    gather x6, local copies, waits for them, and re-layouts, band_matrix(): picked = jnp.take(tap_rows, jnp.clip(offsets, 0, LM - 1), axis=1)  444 us
    reduce_scatter x1, waiting for transfers between devices, per_device(): lax.psum_scatter(product.reshape(lax.axis_size('seq') * row_share, 3, loc...  150 us
    psum x1, waiting for transfers between devices, per_device(): lax.psum(partial_grad.astype(jnp.bfloat16), 'tp').astype(jnp.float32)  121 us
    all_gather x1, blocking collectives, per_device(): lax.all_gather(norm_gain, 'tp', axis=0, tiled=True)  21.9 us
    unnamed x22, local copies, waits for them, and re-layouts  20.8 us
  transfers between devices with their start and end apart: 5, of which 4 were waited for; matrix products, arithmetic and copies ran while one was open for 57% of the time, Pallas kernels for 0%

commit v1 on v0

--- a/solution.py
+++ b/solution.py
@@ -117,7 +117,9 @@
     own_width = width // tp_count
     own_scaled = activations.astype(jnp.float32) * inv_rms
     own_gain = norm_gain.astype(jnp.float32)
-    whole_grad = lax.psum(partial_grad.astype(jnp.bfloat16), "tp").astype(jnp.float32)
+    whole_grad = jnp.sum(lax.all_gather(partial_grad.astype(jnp.bfloat16), "tp"), axis=0).astype(
+        jnp.float32
+    )
     stat = jnp.mean(gain_float * whole_grad * act_float, axis=1, keepdims=True) * inv_rms
     grad_slice = lax.dynamic_slice_in_dim(
         whole_grad, lax.axis_index("tp") * own_width, own_width, 1

time: 849 us -> 1050 us (1.24)
  waiting for transfers between devices: 279 us -> 453 us
  other arithmetic: 12.1 us -> 37.1 us
    all_gather x0 -> x1, waiting for transfers between devices: none -> 321 us  [per_device(): lax.all_gather(partial_grad.astype(jnp.bfloat16), 'tp')]
    psum x1 -> x0, waiting for transfers between devices: 121 us -> none  [per_device(): lax.psum(partial_grad.astype(jnp.bfloat16), 'tp').astype(jnp.float32)]
    reduce_scatter x1, waiting for transfers between devices: 150 us -> 124 us  [per_device(): lax.psum_scatter(product.reshape(lax.axis_size('seq') * row_share, 3, loc...]
    reduce_sum x0 -> x1, other arithmetic: none -> 25 us  [per_device(): jnp.sum(lax.all_gather(partial_grad.astype(jnp.bfloat16), 'tp'), axis=0)]
  transfers between devices with their start and end apart: 5 -> 5, of which waited for: 4 -> 4; matrix products, arithmetic and copies ran while one was open for 57% -> 48% of each run, Pallas kernels for 0% -> 0%
where the time goes in v1:
time: 1050 us
  local copies, waits for them, and re-layouts  469 us (45%)
  waiting for transfers between devices  453 us (43%)
  matrix products  48.7 us (5%)
  other arithmetic  37.1 us (4%)
  blocking collectives  21.9 us (2%)
  between operations  14.1 us (1%)
    gather x6, local copies, waits for them, and re-layouts, band_matrix(): picked = jnp.take(tap_rows, jnp.clip(offsets, 0, LM - 1), axis=1)  446 us
    all_gather x1, waiting for transfers between devices, per_device(): lax.all_gather(partial_grad.astype(jnp.bfloat16), 'tp')  321 us
    reduce_scatter x1, waiting for transfers between devices, per_device(): lax.psum_scatter(product.reshape(lax.axis_size('seq') * row_share, 3, loc...  124 us
    reduce_sum x1, other arithmetic, per_device(): jnp.sum(lax.all_gather(partial_grad.astype(jnp.bfloat16), 'tp'), axis=0)  25 us
    all_gather x1, blocking collectives, per_device(): lax.all_gather(norm_gain, 'tp', axis=0, tiled=True)  21.9 us
  transfers between devices with their start and end apart: 5, of which 4 were waited for; matrix products, arithmetic and copies ran while one was open for 48% of the time, Pallas kernels for 0%

profile of v1, /device:TPU:1, one launch (start us, length us, event | category | flops | bytes accessed | tf_op | source)
XLA Modules:
  0.0 1047.8 jit_solution(448735685374157030)
XLA Ops:
  9.0 16.7 %copy.82 = bf16[8192,3,256]{0,2,1:T(8,128)(2,1)} copy(bf16[8192,3,256]{2,0,1:T(8,128)(2,1)} %param.8) | data formatting | bytes 25165824 | tf_op args[2]
  25.7 21.9 %all-gather.1 = bf16[16,1,512]{2,1,0:T(2,128)(2,1)S(1)} all-gather(bf16[1,1,512]{2,1,0:T(2,128)(2,1)S(1)} %reshape.190), channel_id=1, replica_groups=mesh['seq'=8,'tp'=16] {'tp'}, dimensions={0}, use_global_device_ids=true | all-gather | bytes 17408 | tf_op jit(solution)/shard_map/all_gather | solution.py:54
  48.3 180.4 %gather_fusion = f32[98048,16]{1,0:T(8,128)} fusion(f32[16,128]{0,1:T(8,128)S(1)} %copy.88, s32[98304]{0:T(1024)S(1)} %pad_clamp_fusion.1), kind=kCustom, calls=%fused_computation | custom fusion | bytes 12942336 | tf_op jit(solution)/shard_map/jit(_take)/gather | solution.py:40
  228.7 27.7 %copy.89 = f32[98048,16]{0,1:T(8,128)} copy(f32[98048,16]{1,0:T(8,128)} %gather_fusion) | data formatting | bytes 12550144 | tf_op jit(solution)/shard_map/jit(_take)/gather | solution.py:40
  256.4 10.9 %reshape.176 = f32[256,383,16]{1,0,2:T(8,128)} reshape(f32[98048,16]{0,1:T(8,128)} %copy.89) | data formatting | bytes 12550144 | tf_op jit(solution)/shard_map/jit(_take)/gather | solution.py:40
  268.0 183.3 %gather_fusion.1 = f32[99330,16]{1,0:T(8,128)} fusion(f32[16,128]{0,1:T(8,128)S(1)} %copy.88, s32[100352]{0:T(1024)S(1)} %pad_clamp_fusion), kind=kCustom, calls=%fused_computation.1 | custom fusion | bytes 13111560 | tf_op jit(solution)/shard_map/jit(_take)/gather | solution.py:40
  451.2 28.0 %copy.96 = f32[99330,16]{0,1:T(8,128)} copy(f32[99330,16]{1,0:T(8,128)} %gather_fusion.1) | data formatting | bytes 12714240 | tf_op jit(solution)/shard_map/jit(_take)/gather | solution.py:40
  479.2 15.5 %reshape.184 = f32[258,385,16]{1,0,2:T(8,128)} reshape(f32[99330,16]{0,1:T(8,128)} %copy.96) | data formatting | bytes 12714240 | tf_op jit(solution)/shard_map/jit(_take)/gather | solution.py:40
  494.9 3.1 fusion.5
  498.0 9.4 convolution_convert_fusion.1
  508.1 3.1 collective-permute-start
  511.3 2.9 collective-permute-done
  515.4 6.4 fusion.9
  522.6 1.3 collective-permute-start.1
  524.5 5.1 collective-permute-done.1
  530.2 8.0 fusion.1
  539.1 14.5 %fusion = bf16[256,8192]{1,0:T(8,128)(2,1)} fusion(bf16[256,3,256]{0,2,1:T(8,128)(2,1)S(1)} %add_convert_fusion, bf16[8192,3,256]{2,0,1:T(8,128)(2,1)} %param.8), kind=kOutput, calls=%fused_computation.7 | convolution fusion | flops 3223322624 | bytes 17170432 | tf_op jit(solution)/shard_map/dot_general | solution.py:113
  553.6 10.4 convolution_convert_fusion
  564.8 320.6 %all-gather.7.cloned.1.call-done = bf16[4096,8192]{1,0:T(8,128)(2,1)} async-done(((bf16[256,8192]{1,0:T(8,128)(2,1)}), bf16[4096,8192]{1,0:T(8,128)(2,1)}) %all-gather.7.cloned.1.call-update) | async-done | bytes 67108880 | tf_op jit(solution)/shard_map/all_gather | solution.py:120
  885.4 25.0 %reduce_sum.31 = bf16[256,8192]{1,0:T(8,128)(2,1)} reduce(bf16[16,256,8192]{2,1,0:T(8,128)(2,1)} %bitcast.29, bf16[]{:T(256)} %constant.30.clone.1), dimensions={0}, to_apply=%region_1.2 | reduce | flops 31457280 | bytes 71303168 | tf_op jit(solution)/shard_map/reduce_sum | solution.py:120
  910.4 3.3 convert_element_type.150
  913.9 1.3 copy-done.1
  915.2 1.7 fusion.8
  917.7 123.6 %reduce-scatter.2.cloned.1.call-done = bf16[1024,3,256]{2,0,1:T(8,128)(2,1)} async-done(((bf16[8192,3,256]{2,0,1:T(8,128)(2,1)}), bf16[1024,3,256]{2,0,1:T(8,128)(2,1)}) %reduce-scatter.2.cloned.1.call-update) | async-done | bytes 1572880 | tf_op jit(solution)/shard_map/reduce_scatter | solution.py:133
  (75 shorter events, 9.9 us)
Async XLA Ops:
  7.2 487.7 %all-gather.5.cloned.1.call-start = ((), (), s32[]{:S(2)}) async-start(), calls=%async_computation.1 | async-start | bytes 4456448 | tf_op jit(solution)/shard_map/all_gather | solution.py:53
  7.9 877.5 %all-gather.7.cloned.1.call-start = ((), (), s32[]{:S(2)}) async-start(), calls=%async_computation.3 | async-start | bytes 71303168 | tf_op jit(solution)/shard_map/all_gather | solution.py:120
  9.0 16.7 %copy-start.5 = (bf16[512]{0:T(512)(128)(2,1)S(1)}, bf16[512]{0:T(512)(128)(2,1)}, u32[]{:S(2)}) copy-start(bf16[512]{0:T(512)(128)(2,1)} %param.7) | copy-start | bytes 3076
  9.0 38.7 %copy-start.4 = (f32[16,128]{1,0:T(8,128)S(1)}, f32[16,128]{1,0:T(8,128)}, u32[]{:S(2)}) copy-start(f32[16,128]{1,0:T(8,128)} %param.10) | copy-start | bytes 24580
  479.2 15.6 %copy-start.3 = (f32[3,3,256]{2,1,0:T(4,128)S(1)}, f32[3,3,256]{2,1,0:T(4,128)}, u32[]{:S(2)}) copy-start(f32[3,3,256]{2,1,0:T(4,128)} %param.9) | copy-start | bytes 27652
  508.1 6.0 collective-permute-start
  522.6 7.0 collective-permute-start.1
  553.5 487.8 %reduce-scatter.2.cloned.1.call-start = ((), (), s32[]{:S(2)}) async-start(), calls=%async_computation.2 | async-start | bytes 14155776 | tf_op jit(solution)/shard_map/reduce_scatter | solution.py:133
  910.4 3.5 copy-start
  910.4 4.8 copy-start.1
  910.4 6.5 copy-start.2
Sparse Core Ops, SparseCore 0:
  9.7 41.0 all-gather.4
  553.7 331.6 all-gather.6
  889.9 151.3 reduce-scatter.1
